TPU v7x, 128 devices: a whole 4x4x4 slice. The times are simulated.
128 devices in a mesh: hst: 16 (over z, x), doc: 8 (over y, core).
Axes of the slice: x: 4, y: 4, z: 4, core: 2. Of those that a mesh axis runs over, the one named last changes fastest.
Arguments:
- docs: bfloat16 [1048576, 768], P(('hst', 'doc')), may hold values from -400 to 400, as said below
- w_in: bfloat16 [768, 256], replicated, may hold values from -0.21875 to 0.21875
- w_out: bfloat16 [256, 64], replicated, may hold values from -0.375 to 0.375
- doc_host: int32 [1048576], P(('hst', 'doc')), may hold values from 0 to 2047
- tiles: bfloat16 [8192, 128, 128], P(('hst', 'doc')), may hold values from 0 to 10, as said below
- dst_block: int32 [8192], P(('hst', 'doc')), may hold values from 0 to 15
- src_block: int32 [8192], P(('hst', 'doc')), may hold values from 0 to 255
- tile_count: int32 [128], P(('hst', 'doc')), may hold values from 1 to 64, as said below
- teleport: int32 [32768], P('hst'), may hold values 0 or 1
Outputs:
- scores: float32 [32768, 64], P(('hst', 'doc'))
Inputs may be any that keep to these rules, and one draw needn't show every extreme that they name: `docs`: embeddings stay in the stated range. `tiles`: link weights are nonnegative. `tile_count`: some device uses all 64 slots.
All inputs are finite; a program needn't handle non-finite values. No bound on the sum of `teleport` on one device may be relied on, other than what follows from the above.
Results may differ from a plain program's by a relative error of at most 0.00066.
Values may be sent and summed in bfloat16 or wider, within the bound.
A program may use at most 128 MiB of HBM per device.

v0:
```python
import jax
import jax.numpy as jnp
from jax import lax
from jax.sharding import PartitionSpec as P

HOPS = 3


def body(docs, w_in, w_out, doc_host, tiles, dst_block, src_block, tile_count, teleport):
    host_dev = teleport.shape[0]
    block = tiles.shape[1]
    topics = w_out.shape[1]
    slots = tiles.shape[0]
    hosts_all = host_dev * lax.axis_size("hst")
    nblocks = hosts_all // block
    hidden = jax.nn.gelu(
        jnp.dot(docs, w_in, preferred_element_type=jnp.float32), approximate=True
    ).astype(jnp.bfloat16)
    probs = jax.nn.softmax(jnp.dot(hidden, w_out, preferred_element_type=jnp.float32), axis=-1)
    local_topic = jax.ops.segment_sum(probs, doc_host, num_segments=host_dev)
    used = (jnp.arange(slots) < tile_count[0]).astype(jnp.float32)
    colsum = jnp.sum(tiles, axis=1, dtype=jnp.float32)
    src_onehot = (src_block[:, None] == jnp.arange(nblocks)[None, :]).astype(jnp.float32) * used[
        :, None
    ]
    degree_blocks = jnp.dot(src_onehot.T, colsum, precision=lax.Precision.HIGHEST)
    degree = lax.psum(degree_blocks, ("hst", "doc")).reshape(hosts_all)
    own_degree = lax.dynamic_slice_in_dim(degree, lax.axis_index("hst") * host_dev, host_dev)
    inverse = 1.0 / jnp.maximum(own_degree, 1.0)
    dst_onehot = (dst_block[:, None] == jnp.arange(host_dev // block)[None, :]).astype(
        jnp.float32
    ) * used[:, None]
    member = teleport.astype(jnp.float32)
    rows = host_dev // lax.axis_size("doc")
    host_topic = lax.psum(local_topic, "doc")
    mass = lax.psum(jnp.sum(member[:, None] * host_topic, axis=0), "hst")
    tele = member[:, None] * host_topic / mass
    state = tele
    for hop in range(HOPS):
        sent = (state * inverse[:, None]).astype(jnp.bfloat16)
        full = lax.all_gather(sent, "hst", axis=0, tiled=True)
        slabs = full.reshape(nblocks, block, topics)[src_block]
        prod = jnp.einsum("kij,kjt->kit", tiles, slabs, preferred_element_type=jnp.float32)
        gathered = jnp.einsum("kb,kit->bit", dst_onehot, prod, precision=lax.Precision.HIGHEST)
        inflow = lax.psum(gathered.reshape(host_dev, topics), "doc")
        state = 0.85 * inflow + 0.15 * tele
    result = lax.dynamic_slice_in_dim(state, lax.axis_index("doc") * rows, rows)
    return hosts_all * result


def solution(mesh):
    placed = (
        P(("hst", "doc"), None),
        P(),
        P(),
        P(("hst", "doc")),
        P(("hst", "doc"), None, None),
        P(("hst", "doc")),
        P(("hst", "doc")),
        P(("hst", "doc")),
        P("hst"),
    )
    return jax.shard_map(
        body, mesh=mesh, in_specs=placed, out_specs=P(("hst", "doc"), None), check_vma=False
    )
```

profile of v0, /device:TPU:0, one launch (start us, length us, event | category | flops | bytes accessed | tf_op | source)
XLA Modules:
  0.0 640.4 jit_solution(17008999515403632906)
XLA Ops:
  7.3 2.1 convert_reduce_fusion
  11.2 8.6 %fusion.48 = (f32[8192]{0:T(1024)S(1)}, f32[8192,64]{0,1:T(8,128)S(1)}) fusion(bf16[256,64]{0,1:T(8,128)(2,1)} %param.11, bf16[8192,768]{1,0:T(8,128)(2,1)} %param.9, bf16[768,256]{1,0:T(8,128)(2,1)S(1)} %copy-done), kind=kOutput, calls=%fused_computation.78 | convolution fusion | flops 3509051392 | bytes 15138816 | tf_op jit(solution)/shard_map/dot_general | solution.py:19
  21.6 1.9 fusion.16
  23.5 2.7 copy.18
  26.2 44.5 %scatter_custom_fusion = f32[2048,64]{1,0:T(8,128)S(1)} fusion(s32[8192]{0:T(1024)} %param.12, f32[8192,64]{1,0:T(8,128)} %copy.18, f32[]{:T(128)} %constant.16.clone.1), kind=kCustom, calls=%fused_computation.37 | custom fusion | flops 524288 | bytes 524800 | tf_op jit(solution)/shard_map/scatter-add | solution.py:20
  72.0 82.8 %all-reduce.8.cloned.1.call-done = f32[32768]{0:T(1024)} async-done(((f32[32768]{0:T(1024)}), f32[32768]{0:T(1024)}) %all-reduce.8.cloned.1.call-update) | async-done | bytes 131088 | tf_op jit(solution)/shard_map/psum | solution.py:27
  155.5 59.7 %all-reduce.6.cloned.1.call-done = f32[2048,64]{0,1:T(8,128)} async-done(((f32[2048,64]{0,1:T(8,128)}), f32[2048,64]{0,1:T(8,128)}) %all-reduce.6.cloned.1.call-update) | async-done | bytes 524304 | tf_op jit(solution)/shard_map/psum | solution.py:35
  216.4 40.5 %psum.43 = f32[64]{0:T(128)S(1)} all-reduce(f32[64]{0:T(128)S(1)} %multiply_reduce_fusion), channel_id=1, replica_groups=mesh['hst'=16,'doc'=8] {'hst'}, use_global_device_ids=true, to_apply=%region_5.0 | all-reduce | flops 64 | bytes 512 | tf_op jit(solution)/shard_map/psum | solution.py:36
  259.7 44.7 %all-gather.4.cloned.1.call-done = bf16[32768,64]{0,1:T(8,128)(2,1)} async-done(((bf16[2048,64]{0,1:T(8,128)(2,1)}), bf16[32768,64]{0,1:T(8,128)(2,1)}) %all-gather.4.cloned.1.call-update) | async-done | bytes 4194320 | tf_op jit(solution)/shard_map/all_gather | solution.py:41
  304.4 5.4 copy_bitcast_fusion.2
  309.8 3.2 gather_fusion
  314.6 2.2 fusion.14
  317.8 60.4 %all-reduce.10.cloned.1.call-done = f32[2048,64]{0,1:T(8,128)} async-done(((f32[2048,64]{0,1:T(8,128)}), f32[2048,64]{0,1:T(8,128)}) %all-reduce.10.cloned.1.call-update) | async-done | bytes 524304 | tf_op jit(solution)/shard_map/psum | solution.py:45
  378.3 2.2 multiply_convert_fusion.1
  380.6 51.0 %all-gather.6.cloned.1.call-done = bf16[32768,64]{0,1:T(8,128)(2,1)} async-done(((bf16[2048,64]{0,1:T(8,128)(2,1)}), bf16[32768,64]{0,1:T(8,128)(2,1)}) %all-gather.6.cloned.1.call-update) | async-done | bytes 4194320 | tf_op jit(solution)/shard_map/all_gather | solution.py:41
  431.6 5.4 copy_bitcast_fusion.1
  436.9 3.1 gather_fusion.1
  441.6 2.2 fusion.12
  444.8 60.4 %all-reduce.12.cloned.1.call-done = f32[2048,64]{0,1:T(8,128)} async-done(((f32[2048,64]{0,1:T(8,128)}), f32[2048,64]{0,1:T(8,128)}) %all-reduce.12.cloned.1.call-update) | async-done | bytes 524304 | tf_op jit(solution)/shard_map/psum | solution.py:45
  507.4 51.0 %all-gather.8.cloned.1.call-done = bf16[32768,64]{0,1:T(8,128)(2,1)} async-done(((bf16[2048,64]{0,1:T(8,128)(2,1)}), bf16[32768,64]{0,1:T(8,128)(2,1)}) %all-gather.8.cloned.1.call-update) | async-done | bytes 4194320 | tf_op jit(solution)/shard_map/all_gather | solution.py:41
  558.4 5.4 copy_bitcast_fusion
  563.7 3.1 gather_fusion.2
  568.3 2.2 fusion.10
  571.6 60.5 %all-reduce.14.cloned.1.call-done = f32[2048,64]{0,1:T(8,128)} async-done(((f32[2048,64]{0,1:T(8,128)}), f32[2048,64]{0,1:T(8,128)}) %all-reduce.14.cloned.1.call-update) | async-done | bytes 524304 | tf_op jit(solution)/shard_map/psum | solution.py:45
  (62 shorter events, 20.6 us)
Async XLA Ops:
  6.5 4.7 copy-start
  6.5 148.3 %all-reduce.8.cloned.1.call-start = ((), (), s32[]{:S(2)}) async-start(), calls=%async_computation.1 | async-start | bytes 262144 | tf_op jit(solution)/shard_map/psum | solution.py:27
  7.3 2.1 copy-start.5
  11.2 204.0 %all-reduce.6.cloned.1.call-start = ((), (), s32[]{:S(2)}) async-start(), calls=%async_computation | async-start | bytes 1048576 | tf_op jit(solution)/shard_map/psum | solution.py:35
  19.9 1.3 copy-start.2
  23.5 48.5 %copy-start.8 = (s32[2048]{0:T(1024)S(1)}, s32[2048]{0:T(1024)}, u32[]{:S(2)}) copy-start(s32[2048]{0:T(1024)} %param.17) | copy-start | bytes 24580
  23.5 235.5 %copy-start.13 = (s32[64]{0:T(128)S(1)}, s32[64]{0:T(128)}, u32[]{:S(2)}) copy-start(s32[64]{0:T(128)} %param.15) | copy-start | bytes 772
  71.9 232.4 %all-gather.4.cloned.1.call-start = ((), (), s32[]{:S(2)}) async-start(), calls=%async_computation.2 | async-start | bytes 4456448 | tf_op jit(solution)/shard_map/all_gather | solution.py:41
  256.9 47.5 %copy-start.11 = (f32[64]{0:T(128)}, f32[64]{0:T(128)S(1)}, u32[]{:S(2)}) copy-start(f32[64]{0:T(128)S(1)} %psum.43) | copy-start | bytes 772
  258.8 119.5 %all-reduce.10.cloned.1.call-start = ((), (), s32[]{:S(2)}) async-start(), calls=%async_computation.3 | async-start | bytes 1048576 | tf_op jit(solution)/shard_map/psum | solution.py:45
  309.8 3.2 copy-start.1
  313.0 1.6 copy-start.6
  313.0 1.6 copy-start.9
  314.6 63.7 %copy-start.3 = (f32[2048,64]{0,1:T(8,128)S(1)}, f32[2048,64]{0,1:T(8,128)}, u32[]{:S(2)}) copy-start(f32[2048,64]{0,1:T(8,128)} %all-reduce.6.cloned.1.call-done) | copy-start | bytes 1572868
  314.6 63.7 %copy-start.12 = (f32[64]{0:T(128)S(1)}, f32[64]{0:T(128)}, u32[]{:S(2)}) copy-start(f32[64]{0:T(128)} %copy-done.11) | copy-start | bytes 772
  317.8 113.8 %all-gather.6.cloned.1.call-start = ((), (), s32[]{:S(2)}) async-start(), calls=%async_computation.4 | async-start | bytes 4456448 | tf_op jit(solution)/shard_map/all_gather | solution.py:41
  380.5 124.8 %all-reduce.12.cloned.1.call-start = ((), (), s32[]{:S(2)}) async-start(), calls=%async_computation.5 | async-start | bytes 1048576 | tf_op jit(solution)/shard_map/psum | solution.py:45
  436.9 4.6 copy-start.7
  436.9 4.6 copy-start.10
  441.6 63.7 %copy-start.4 = (f32[2048,64]{0,1:T(8,128)S(1)}, f32[2048,64]{0,1:T(8,128)}, u32[]{:S(2)}) copy-start(f32[2048,64]{0,1:T(8,128)} %get-tuple-element.6) | copy-start | bytes 1572868
  444.8 113.6 %all-gather.8.cloned.1.call-start = ((), (), s32[]{:S(2)}) async-start(), calls=%async_computation.6 | async-start | bytes 4456448 | tf_op jit(solution)/shard_map/all_gather | solution.py:41
  507.1 124.9 %all-reduce.14.cloned.1.call-start = ((), (), s32[]{:S(2)}) async-start(), calls=%async_computation.7 | async-start | bytes 1048576 | tf_op jit(solution)/shard_map/psum | solution.py:45
Sparse Core Ops, SparseCore 0:
  12.1 142.6 all-reduce.7
  157.2 57.9 all-reduce.5
  258.9 45.3 all-gather.3
  317.9 60.3 all-reduce.9
  380.6 50.8 all-gather.5
  444.9 60.3 all-reduce.11
  507.4 50.8 all-gather.7
  571.7 60.3 all-reduce.13
where the time goes:
time: 641 us; the launch traced here: 640 us
  waiting for transfers between devices  471 us (73%)
  other arithmetic  58.8 us (9%)
  blocking collectives  40.5 us (6%)
  local copies, waits for them, and re-layouts  33.6 us (5%)
  matrix products  21.7 us (3%)
  between operations  14.4 us (2%)
    psum x3, waiting for transfers between devices, body(): inflow = lax.psum(gathered.reshape(host_dev, topics), 'doc')  181 us
    all_gather x3, waiting for transfers between devices, body(): full = lax.all_gather(sent, 'hst', axis=0, tiled=True)  147 us
    psum x1, waiting for transfers between devices, body(): degree = lax.psum(degree_blocks, ('hst', 'doc')).reshape(hosts_all)  82.8 us
    psum x1, waiting for transfers between devices, body(): host_topic = lax.psum(local_topic, 'doc')  59.7 us
    scatter-add x1, other arithmetic, body(): local_topic = jax.ops.segment_sum(probs, doc_host, num_segments=host_dev)  44.5 us
    psum x1, blocking collectives, body(): mass = lax.psum(jnp.sum(member[:, None] * host_topic, axis=0), 'hst')  40.5 us
    reshape x3, local copies, waits for them, and re-layouts, body(): slabs = full.reshape(nblocks, block, topics)[src_block]  16.1 us
  transfers between devices with their start and end apart: 8, of which 8 were waited for; matrix products, arithmetic and copies ran while one was open for 9% of the time, Pallas kernels for 0%

commit v1 on v0

--- a/solution.py
+++ b/solution.py
@@ -24,7 +24,7 @@
         :, None
     ]
     degree_blocks = jnp.dot(src_onehot.T, colsum, precision=lax.Precision.HIGHEST)
-    degree = lax.psum(degree_blocks, ("hst", "doc")).reshape(hosts_all)
+    degree = lax.psum(lax.psum(degree_blocks, "hst"), "doc").reshape(hosts_all)
     own_degree = lax.dynamic_slice_in_dim(degree, lax.axis_index("hst") * host_dev, host_dev)
     inverse = 1.0 / jnp.maximum(own_degree, 1.0)
     dst_onehot = (dst_block[:, None] == jnp.arange(host_dev // block)[None, :]).astype(

time: 641 us -> 586 us (0.914)
  waiting for transfers between devices: 471 us -> 416 us
    psum x1, waiting for transfers between devices: 82.8 us -> 24.3 us  [body(): degree = lax.psum(lax.psum(degree_blocks, 'hst'), 'doc').reshape(hosts_all)]
  transfers between devices with their start and end apart: 8 -> 8, of which waited for: 8 -> 8; matrix products, arithmetic and copies ran while one was open for 9% -> 10% of each run, Pallas kernels for 0% -> 0%
where the time goes in v1:
time: 586 us
  waiting for transfers between devices  416 us (71%)
  other arithmetic  58.8 us (10%)
  blocking collectives  40.5 us (7%)
  local copies, waits for them, and re-layouts  33.5 us (6%)
  matrix products  21.7 us (4%)
  between operations  14.4 us (2%)
    psum x3, waiting for transfers between devices, body(): inflow = lax.psum(gathered.reshape(host_dev, topics), 'doc')  181 us
    all_gather x3, waiting for transfers between devices, body(): full = lax.all_gather(sent, 'hst', axis=0, tiled=True)  147 us
    psum x1, waiting for transfers between devices, body(): host_topic = lax.psum(local_topic, 'doc')  63.2 us
    scatter-add x1, other arithmetic, body(): local_topic = jax.ops.segment_sum(probs, doc_host, num_segments=host_dev)  44.5 us
    psum x1, blocking collectives, body(): mass = lax.psum(jnp.sum(member[:, None] * host_topic, axis=0), 'hst')  40.5 us
    psum x1, waiting for transfers between devices, body(): degree = lax.psum(lax.psum(degree_blocks, 'hst'), 'doc').reshape(hosts_all)  24.3 us
    reshape x3, local copies, waits for them, and re-layouts, body(): slabs = full.reshape(nblocks, block, topics)[src_block]  16.1 us
  transfers between devices with their start and end apart: 8, of which 8 were waited for; matrix products, arithmetic and copies ran while one was open for 10% of the time, Pallas kernels for 0%

profile of v1, /device:TPU:0, one launch (start us, length us, event | category | flops | bytes accessed | tf_op | source)
XLA Modules:
  0.0 585.6 jit_solution(5722746378023377082)
XLA Ops:
  7.3 2.1 convert_reduce_fusion
  11.2 8.6 %fusion.49 = (f32[8192]{0:T(1024)S(1)}, f32[8192,64]{0,1:T(8,128)S(1)}) fusion(bf16[256,64]{0,1:T(8,128)(2,1)} %param.11, bf16[8192,768]{1,0:T(8,128)(2,1)} %param.9, bf16[768,256]{1,0:T(8,128)(2,1)S(1)} %copy-done), kind=kOutput, calls=%fused_computation.78 | convolution fusion | flops 3509051392 | bytes 15138816 | tf_op jit(solution)/shard_map/dot_general | solution.py:19
  21.6 1.9 fusion.16
  23.5 2.7 copy.18
  26.2 44.5 %scatter_custom_fusion = f32[2048,64]{1,0:T(8,128)S(1)} fusion(s32[8192]{0:T(1024)} %param.12, f32[8192,64]{1,0:T(8,128)} %copy.18, f32[]{:T(128)} %constant.16.clone.1), kind=kCustom, calls=%fused_computation.36 | custom fusion | flops 524288 | bytes 524800 | tf_op jit(solution)/shard_map/scatter-add | solution.py:20
  71.9 24.3 %all-reduce.7.cloned.1.call-done = f32[256,128]{1,0:T(8,128)} async-done(((f32[256,128]{1,0:T(8,128)}), f32[256,128]{1,0:T(8,128)}) %all-reduce.7.cloned.1.call-update) | async-done | bytes 131088 | tf_op jit(solution)/shard_map/psum | solution.py:27
  96.3 63.2 %all-reduce.15.cloned.1.call-done = (f32[2048,64]{0,1:T(8,128)}, f32[32768]{0:T(1024)}) async-done(((f32[2048,64]{0,1:T(8,128)}, f32[32768]{0:T(1024)}), (f32[2048,64]{0,1:T(8,128)}, f32[32768]{0:T(1024)})) %all-reduce.15.cloned.1.call-update) | async-done | bytes 655376 | tf_op jit(solution)/shard_map/psum | solution.py:35
  160.7 40.5 %psum.50 = f32[64]{0:T(128)S(1)} all-reduce(f32[64]{0:T(128)S(1)} %multiply_reduce_fusion), channel_id=1, replica_groups=mesh['hst'=16,'doc'=8] {'hst'}, use_global_device_ids=true, to_apply=%region_5.0 | all-reduce | flops 64 | bytes 512 | tf_op jit(solution)/shard_map/psum | solution.py:36
  204.7 44.7 %all-gather.4.cloned.1.call-done = bf16[32768,64]{0,1:T(8,128)(2,1)} async-done(((bf16[2048,64]{0,1:T(8,128)(2,1)}), bf16[32768,64]{0,1:T(8,128)(2,1)}) %all-gather.4.cloned.1.call-update) | async-done | bytes 4194320 | tf_op jit(solution)/shard_map/all_gather | solution.py:41
  249.4 5.4 copy_bitcast_fusion.2
  254.8 3.2 gather_fusion
  259.6 2.2 fusion.14
  262.8 60.4 %all-reduce.9.cloned.1.call-done = f32[2048,64]{0,1:T(8,128)} async-done(((f32[2048,64]{0,1:T(8,128)}), f32[2048,64]{0,1:T(8,128)}) %all-reduce.9.cloned.1.call-update) | async-done | bytes 524304 | tf_op jit(solution)/shard_map/psum | solution.py:45
  323.3 2.2 multiply_convert_fusion.1
  325.5 51.0 %all-gather.6.cloned.1.call-done = bf16[32768,64]{0,1:T(8,128)(2,1)} async-done(((bf16[2048,64]{0,1:T(8,128)(2,1)}), bf16[32768,64]{0,1:T(8,128)(2,1)}) %all-gather.6.cloned.1.call-update) | async-done | bytes 4194320 | tf_op jit(solution)/shard_map/all_gather | solution.py:41
  376.5 5.4 copy_bitcast_fusion.1
  381.9 3.1 gather_fusion.1
  386.6 2.2 fusion.12
  389.8 60.5 %all-reduce.11.cloned.1.call-done = f32[2048,64]{0,1:T(8,128)} async-done(((f32[2048,64]{0,1:T(8,128)}), f32[2048,64]{0,1:T(8,128)}) %all-reduce.11.cloned.1.call-update) | async-done | bytes 524304 | tf_op jit(solution)/shard_map/psum | solution.py:45
  452.4 51.2 %all-gather.8.cloned.1.call-done = bf16[32768,64]{0,1:T(8,128)(2,1)} async-done(((bf16[2048,64]{0,1:T(8,128)(2,1)}), bf16[32768,64]{0,1:T(8,128)(2,1)}) %all-gather.8.cloned.1.call-update) | async-done | bytes 4194320 | tf_op jit(solution)/shard_map/all_gather | solution.py:41
  503.6 5.4 copy_bitcast_fusion
  508.9 3.1 gather_fusion.2
  513.5 2.2 fusion.10
  516.8 60.5 %all-reduce.13.cloned.1.call-done = f32[2048,64]{0,1:T(8,128)} async-done(((f32[2048,64]{0,1:T(8,128)}), f32[2048,64]{0,1:T(8,128)}) %all-reduce.13.cloned.1.call-update) | async-done | bytes 524304 | tf_op jit(solution)/shard_map/psum | solution.py:45
  (62 shorter events, 20.5 us)
Async XLA Ops:
  6.5 4.7 copy-start
  6.5 89.7 %all-reduce.7.cloned.1.call-start = ((), (), s32[]{:S(2)}) async-start(), calls=%async_computation | async-start | bytes 262144 | tf_op jit(solution)/shard_map/psum | solution.py:27
  7.3 2.1 copy-start.5
  11.2 148.4 %all-reduce.15.cloned.1.call-start = ((), (), s32[]{:S(2)}) async-start(), calls=%async_computation.7 | async-start | bytes 1310720 | tf_op jit(solution)/shard_map/psum | solution.py:35
  19.9 1.3 copy-start.2
  23.5 72.8 %copy-start.8 = (s32[2048]{0:T(1024)S(1)}, s32[2048]{0:T(1024)}, u32[]{:S(2)}) copy-start(s32[2048]{0:T(1024)} %param.17) | copy-start | bytes 24580
  23.5 180.6 %copy-start.13 = (s32[64]{0:T(128)S(1)}, s32[64]{0:T(128)}, u32[]{:S(2)}) copy-start(s32[64]{0:T(128)} %param.15) | copy-start | bytes 772
  96.2 153.2 %all-gather.4.cloned.1.call-start = ((), (), s32[]{:S(2)}) async-start(), calls=%async_computation.1 | async-start | bytes 4456448 | tf_op jit(solution)/shard_map/all_gather | solution.py:41
  201.3 48.1 %copy-start.11 = (f32[64]{0:T(128)}, f32[64]{0:T(128)S(1)}, u32[]{:S(2)}) copy-start(f32[64]{0:T(128)S(1)} %psum.50) | copy-start | bytes 772
  203.8 119.4 %all-reduce.9.cloned.1.call-start = ((), (), s32[]{:S(2)}) async-start(), calls=%async_computation.2 | async-start | bytes 1048576 | tf_op jit(solution)/shard_map/psum | solution.py:45
  254.8 3.2 copy-start.1
  258.0 1.6 copy-start.6
  258.0 1.6 copy-start.9
  259.6 63.7 %copy-start.3 = (f32[2048,64]{0,1:T(8,128)S(1)}, f32[2048,64]{0,1:T(8,128)}, u32[]{:S(2)}) copy-start(f32[2048,64]{0,1:T(8,128)} %get-tuple-element.5) | copy-start | bytes 1572868
  259.6 63.7 %copy-start.12 = (f32[64]{0:T(128)S(1)}, f32[64]{0:T(128)}, u32[]{:S(2)}) copy-start(f32[64]{0:T(128)} %copy-done.11) | copy-start | bytes 772
  262.8 113.7 %all-gather.6.cloned.1.call-start = ((), (), s32[]{:S(2)}) async-start(), calls=%async_computation.3 | async-start | bytes 4456448 | tf_op jit(solution)/shard_map/all_gather | solution.py:41
  325.5 124.8 %all-reduce.11.cloned.1.call-start = ((), (), s32[]{:S(2)}) async-start(), calls=%async_computation.4 | async-start | bytes 1048576 | tf_op jit(solution)/shard_map/psum | solution.py:45
  381.9 4.6 copy-start.7
  381.9 4.6 copy-start.10
  386.5 63.7 %copy-start.4 = (f32[2048,64]{0,1:T(8,128)S(1)}, f32[2048,64]{0,1:T(8,128)}, u32[]{:S(2)}) copy-start(f32[2048,64]{0,1:T(8,128)} %get-tuple-element.8) | copy-start | bytes 1572868
  389.8 113.8 %all-gather.8.cloned.1.call-start = ((), (), s32[]{:S(2)}) async-start(), calls=%async_computation.5 | async-start | bytes 4456448 | tf_op jit(solution)/shard_map/all_gather | solution.py:41
  452.1 125.1 %all-reduce.13.cloned.1.call-start = ((), (), s32[]{:S(2)}) async-start(), calls=%async_computation.6 | async-start | bytes 1048576 | tf_op jit(solution)/shard_map/psum | solution.py:45
Sparse Core Ops, SparseCore 0:
  11.3 84.8 all-reduce.6
  98.8 60.6 all-reduce.14
  204.0 45.3 all-gather.3
  262.9 60.3 all-reduce.8
  325.6 50.8 all-gather.5
  389.9 60.3 all-reduce.10
  452.6 50.8 all-gather.7
  516.9 60.3 all-reduce.12
